TPU v7x, 32 devices: a whole 2x2x4 slice. The times are simulated.
32 devices in a mesh: seq: 8 (over y, x, core), head: 4 (over z).
Axes of the slice: x: 2, y: 2, z: 4, core: 2. Of those that a mesh axis runs over, the one named last changes fastest.
Arguments:
- queries: bfloat16 [4096, 2048], P(('seq', 'head')), may hold values from -6 to 6
- keys: bfloat16 [4096, 2048], P(('seq', 'head')), may hold values from -6 to 6
- values: bfloat16 [4096, 2048], P(('seq', 'head')), may hold values from -6 to 6
- log_decay: bfloat16 [4096, 16], P(('seq', 'head')), may hold values from -0.6 to 0, as said below
- out_weight: bfloat16 [2048, 2048], P(('seq', 'head')), may hold values from -0.125 to 0.125
Outputs:
- mixed_out: bfloat16 [4096, 2048], P(('seq', 'head'))
Inputs may be any that keep to these rules, and one draw needn't show every extreme that they name: `log_decay`: every entry is at most zero.
All inputs are finite; a program needn't handle non-finite values.
Results may differ from a plain program's by a relative error of at most 0.0054.
Values may be sent and summed in bfloat16 or wider, within the bound.
A program may use at most 64 MiB of HBM per device.

v0:
```python
import jax
import jax.numpy as jnp
from jax import lax
from jax.sharding import PartitionSpec as P

SPAN = 256


def entering(x, axis, combine, identity):
    count, place = (lax.axis_size(axis), lax.axis_index(axis))
    everything = jax.tree.map(lambda part: lax.all_gather(part, axis), x)
    start = jax.tree.map(
        lambda part, zero: jnp.broadcast_to(jnp.asarray(zero, part.dtype), part.shape), x, identity
    )

    def turn(k, before):
        reached = k < place
        new = combine(before, jax.tree.map(lambda part: part[k], everything))
        return jax.tree.map(lambda a, b: jnp.where(reached, a, b), new, before)

    return lax.fori_loop(0, count, turn, start)


def local(queries, keys, values, log_decay, out_weight):
    queries_loc, keys_loc, values_loc, decay_loc = (
        lax.all_to_all(queries, "head", split_axis=1, concat_axis=0, tiled=True),
        lax.all_to_all(keys, "head", split_axis=1, concat_axis=0, tiled=True),
        lax.all_to_all(values, "head", split_axis=1, concat_axis=0, tiled=True),
        lax.all_to_all(log_decay, "head", split_axis=1, concat_axis=0, tiled=True),
    )
    shard_rows = queries_loc.shape[0]
    head_count = decay_loc.shape[1]
    head_dim = queries_loc.shape[1] // head_count
    block_count = shard_rows // SPAN
    queries_blk = queries_loc.reshape(block_count, SPAN, head_count, head_dim)
    keys_blk = keys_loc.reshape(block_count, SPAN, head_count, head_dim)
    values_blk = values_loc.reshape(block_count, SPAN, head_count, head_dim)
    within = jnp.cumsum(
        decay_loc.reshape(block_count, SPAN, head_count).astype(jnp.float32), axis=1
    )
    block_decay = within[:, -1, :]
    within_t = jnp.transpose(within, (0, 2, 1))
    causal = lax.broadcasted_iota(jnp.int32, (SPAN, SPAN), 0) >= lax.broadcasted_iota(
        jnp.int32, (SPAN, SPAN), 1
    )
    differences = within_t[:, :, :, None] - within_t[:, :, None, :]
    decay_mask = jnp.exp(jnp.where(causal[None, None], differences, -jnp.inf))
    scores = jnp.einsum(
        "nthd,nshd->nhts", queries_blk, keys_blk, preferred_element_type=jnp.float32
    )
    weights = (scores * decay_mask).astype(jnp.bfloat16)
    local_part = jnp.einsum(
        "nhts,nshd->nthd", weights, values_blk, preferred_element_type=jnp.float32
    )
    scaled_keys = (
        jnp.exp(block_decay[:, None, :] - within)[..., None] * keys_blk.astype(jnp.float32)
    ).astype(jnp.bfloat16)
    block_state = jnp.einsum(
        "nshd,nshe->nhde", scaled_keys, values_blk, preferred_element_type=jnp.float32
    )
    decay_incl = jnp.cumsum(block_decay, axis=0)
    decay_excl = decay_incl - block_decay
    block_index = lax.broadcasted_iota(jnp.int32, (block_count, block_count), 0)
    earlier_blocks = block_index > lax.broadcasted_iota(jnp.int32, (block_count, block_count), 1)
    pair_gaps = decay_excl[:, None, :] - decay_incl[None, :, :]
    block_weights = jnp.exp(jnp.where(earlier_blocks[:, :, None], pair_gaps, -jnp.inf))
    prior_states = jnp.einsum(
        "cjh,jhde->chde", block_weights, block_state, precision=lax.Precision.HIGHEST
    )
    total_decay = decay_incl[-1]
    final_state = jnp.einsum(
        "jh,jhde->hde",
        jnp.exp(total_decay[None, :] - decay_incl),
        block_state,
        precision=lax.Precision.HIGHEST,
    )

    def link(earlier, later):
        return (jnp.exp(later[1])[:, None, None] * earlier[0] + later[0], earlier[1] + later[1])

    incoming, _ = entering(
        (final_state, total_decay),
        "seq",
        link,
        (jnp.zeros_like(final_state), jnp.zeros_like(total_decay)),
    )
    full_states = prior_states + jnp.exp(decay_excl)[:, :, None, None] * incoming[None]
    scaled_queries = queries_blk.astype(jnp.float32) * jnp.exp(within)[..., None]
    carried_part = jnp.einsum(
        "nthd,nhde->nthe", scaled_queries, full_states, precision=lax.Precision.HIGHEST
    )
    combined = local_part + carried_part
    normed = (
        combined * lax.rsqrt(jnp.mean(combined * combined, axis=-1, keepdims=True) + 1e-05)
    ).astype(jnp.bfloat16)
    normed = normed.reshape(shard_rows, head_count * head_dim)
    restored = lax.all_to_all(normed, "head", split_axis=0, concat_axis=1, tiled=True)
    projected = jnp.dot(
        restored,
        lax.all_gather(out_weight, ("seq", "head"), axis=0, tiled=True),
        preferred_element_type=jnp.float32,
    )
    return projected.astype(jnp.bfloat16)


def solution(mesh):
    placed = (
        P(("seq", "head"), None),
        P(("seq", "head"), None),
        P(("seq", "head"), None),
        P(("seq", "head"), None),
        P(("seq", "head"), None),
    )
    return jax.shard_map(
        local, mesh=mesh, in_specs=placed, out_specs=P(("seq", "head"), None), check_vma=False
    )
```

profile of v0, /device:TPU:0, one launch (start us, length us, event | category | flops | bytes accessed | tf_op | source)
XLA Modules:
  0.0 178.9 jit_solution(6844246718815096049)
XLA Ops:
  6.5 6.4 %all-to-all-start.2 = ((bf16[128,4,4]{0,2,1:T(4,128)(2,1)}), bf16[128,4,4]{0,2,1:T(4,128)(2,1)S(1)}, u32[]{:S(2)}, u32[]{:S(2)}) async-start(bf16[128,4,4]{0,2,1:T(4,128)(2,1)} %bitcast.83), calls=%async_computation.2 | async-start | bytes 8192 | tf_op jit(solution)/shard_map/all_to_all | solution.py:29
  13.0 1.9 %copy.139 = bf16[16,4,8,512]{3,2,0,1:T(8,128)(2,1)} copy(bf16[16,4,8,512]{3,2,1,0:T(8,128)(2,1)} %bitcast.73) | data formatting | bytes 1048576 | tf_op jit(solution)/shard_map/all_to_all | solution.py:27
  14.9 3.7 %all-to-all-done.2 = bf16[128,4,4]{0,2,1:T(4,128)(2,1)S(1)} async-done(((bf16[128,4,4]{0,2,1:T(4,128)(2,1)}), bf16[128,4,4]{0,2,1:T(4,128)(2,1)S(1)}, u32[]{:S(2)}, u32[]{:S(2)}) %all-to-all-start.2) | async-done | bytes 4128 | tf_op jit(solution)/shard_map/all_to_all | solution.py:29
  18.6 3.5 %all-to-all-start.1 = ((bf16[128,4,512]{2,0,1:T(8,128)(2,1)}), bf16[128,4,512]{2,0,1:T(8,128)(2,1)S(1)}, u32[]{:S(2)}, u32[]{:S(2)}) async-start(bf16[128,4,512]{2,0,1:T(8,128)(2,1)} %bitcast.61), calls=%async_computation.1 | async-start | bytes 1048576 | tf_op jit(solution)/shard_map/all_to_all | solution.py:27
  22.9 2.4 %reduce-window.6 = f32[2,4,2,128]{3,2,1,0:T(2,128)S(1)} reduce-window(f32[2,4,2,128]{3,2,1,0:T(2,128)S(1)} %reshape.113, f32[]{:T(128)} %constant.39.clone.1), window={size=1x1x1x128 pad=0_0x0_0x0_0x127_0}, to_apply=%region_0.0 | reduce-window | flops 260096 | bytes 16388 | tf_op jit(solution)/shard_map/reduce-window
  25.7 9.7 %all-to-all-done.1 = bf16[128,4,512]{2,0,1:T(8,128)(2,1)S(1)} async-done(((bf16[128,4,512]{2,0,1:T(8,128)(2,1)}), bf16[128,4,512]{2,0,1:T(8,128)(2,1)S(1)}, u32[]{:S(2)}, u32[]{:S(2)}) %all-to-all-start.1) | async-done | bytes 524320 | tf_op jit(solution)/shard_map/all_to_all | solution.py:27
  35.3 3.5 %all-to-all-start.3 = ((bf16[128,4,512]{2,0,1:T(8,128)(2,1)}), bf16[128,4,512]{2,0,1:T(8,128)(2,1)S(1)}, u32[]{:S(2)}, u32[]{:S(2)}) async-start(bf16[128,4,512]{2,0,1:T(8,128)(2,1)} %bitcast.60), calls=%async_computation.3 | async-start | bytes 1048576 | tf_op jit(solution)/shard_map/all_to_all | solution.py:28
  39.7 13.0 %all-to-all-done.3 = bf16[128,4,512]{2,0,1:T(8,128)(2,1)S(1)} async-done(((bf16[128,4,512]{2,0,1:T(8,128)(2,1)}), bf16[128,4,512]{2,0,1:T(8,128)(2,1)S(1)}, u32[]{:S(2)}, u32[]{:S(2)}) %all-to-all-start.3) | async-done | bytes 524320 | tf_op jit(solution)/shard_map/all_to_all | solution.py:28
  54.6 2.7 %fusion.19 = f32[4,1,128,128]{3,1,2,0:T(1,128)} fusion(f32[2,4,1,1]{0,2,3,1:T(1,128)S(1)} %copy.102, f32[2,4,128,128]{3,2,1,0:T(8,128)S(1)} %fusion.11), kind=kOutput, calls=%fused_computation.30 | convolution fusion | flops 1572864 | bytes 786464 | tf_op jit(solution)/shard_map/jh,jhde->hde/dot_general | solution.py:71
  59.0 3.5 %all-to-all-start = ((bf16[128,4,512]{2,0,1:T(8,128)(2,1)}), bf16[128,4,512]{2,0,1:T(8,128)(2,1)S(1)}, u32[]{:S(2)}, u32[]{:S(2)}) async-start(bf16[128,4,512]{2,0,1:T(8,128)(2,1)} %bitcast.62), calls=%async_computation | async-start | bytes 1048576 | tf_op jit(solution)/shard_map/all_to_all | solution.py:26
  62.6 8.8 %all-gather.1 = f32[8,1,4]{2,1,0:T(1,128)S(1)} all-gather(f32[1,1,4]{2,1,0:T(1,128)S(1)} %get-tuple-element.158), channel_id=1, replica_groups=mesh['seq'=8,'head'=4] {'seq'}, dimensions={0}, use_global_device_ids=true | all-gather | bytes 144 | tf_op jit(solution)/shard_map/all_gather | solution.py:11
  71.9 4.5 %all-to-all-done = bf16[128,4,512]{2,0,1:T(8,128)(2,1)S(1)} async-done(((bf16[128,4,512]{2,0,1:T(8,128)(2,1)}), bf16[128,4,512]{2,0,1:T(8,128)(2,1)S(1)}, u32[]{:S(2)}, u32[]{:S(2)}) %all-to-all-start) | async-done | bytes 524320 | tf_op jit(solution)/shard_map/all_to_all | solution.py:26
  77.2 7.4 %all-gather.7.cloned.1.call-done = f32[32,128,128]{2,1,0:T(8,128)} async-done(((f32[4,128,128]{2,1,0:T(8,128)}), f32[32,128,128]{2,1,0:T(8,128)}) %all-gather.7.cloned.1.call-update) | async-done | bytes 2097168 | tf_op jit(solution)/shard_map/all_gather | solution.py:11
  84.6 8.7 %while.14 = (s32[]{:T(128)}, f32[4,128,128]{2,1,0:T(8,128)S(1)}, s32[]{:T(128)}, f32[8,4]{1,0:T(8,128)S(1)}, f32[8,4,128,128]{3,2,1,0:T(8,128)}, /*index=5*/s32[]{:T(128)}, s32[]{:T(128)}) while((s32[]{:T(128)}, f32[4,128,128]{2,1,0:T(8,128)S(1)}, s32[]{:T(128)}, f32[8,4]{1,0:T(8,128)S(1)}, f32[8,4,128,128]{3,2,1,0:T(8,128)}, ...), condition=%wide.region_4.5_spmd.clone, body=%wide.region_3.4_spmd.clone.sunk | while | flops 262148 | bytes 786585 | solution.py:21
  84.6 1.1 fusion.40
  85.7 1.1 fusion.40
  89.0 1.1 fusion.40
  90.0 1.1 fusion.40
  93.3 2.2 %fusion.4 = f32[2,4,128,128]{3,0,2,1:T(2,128)S(1)} fusion(f32[2,4,128,128]{3,2,1,0:T(8,128)S(1)} %copy-done.1, f32[4,128,128]{2,1,0:T(8,128)S(1)} %get-tuple-element.99, f32[2,4]{0,1:T(4,128)S(1)} %copy.93, pred[2,2]{1,0:T(4,128)(4,1)S(1)} %iota_compare_fusion.1, f32[2,4]{0,1:T(4,128)S(1)} %copy.91, f32[2,4]{0,1:T(4,128)S(1)} %bitcast.84), kind=kOutput, calls=%fused_computation.10 | convolution fusion | flops 3407904 | bytes 1310820 | tf_op jit(solution)/shard_map/cjh,jhde->chde/dot_general | solution.py:67
  95.5 2.2 %convolution_bitcast_fusion = f32[2,256,4,128]{1,3,2,0:T(8,128)} fusion(f32[2,256,4,128]{3,2,1,0:T(4,128)S(1)} %convert_multiply_fusion, f32[2,4,128,128]{3,0,2,1:T(2,128)S(1)} %fusion.4), kind=kOutput, calls=%fused_computation.8 | convolution fusion | flops 402653184 | bytes 2621440 | tf_op jit(solution)/shard_map/nthd,nhde->nthe/dot_general | solution.py:89
  97.7 2.2 %multiply_reduce_fusion = (f32[2,256,4]{1,2,0:T(4,128)S(1)}, f32[2,256,4,128]{1,3,2,0:T(8,128)S(1)}) fusion(f32[2,256,4,128]{1,3,2,0:T(8,128)} %convolution_bitcast_fusion, bf16[2,256,4,128]{3,2,1,0:T(4,128)(2,1)S(1)} %reshape.112, f32[2,4,256]{2,1,0:T(4,128)S(1)} %reduce_window_sum.37, pred[256,256]{1,0:T(8,128)(4,1)S(1)} %iota_compare_fusion, ...), kind=kOutput, calls=%fused_computation.13 | convolution fusion | flops 271316992 | bytes 3751936 | tf_op jit(solution)/shard_map/nhts,nshd->nthd/dot_general | solution.py:52
  100.5 24.3 %all_to_all.80 = bf16[4,128,512]{2,1,0:T(8,128)(2,1)S(1)} all-to-all(bf16[4,128,512]{2,1,0:T(8,128)(2,1)S(1)} %all_to_all.71), channel_id=1, replica_groups=mesh['seq'=8,'head'=4] {'head'}, dimensions={0} | all-to-all | bytes 1048576 | tf_op jit(solution)/shard_map/all_to_all | solution.py:97
  125.1 41.4 %all-gather.5.cloned.1.call-done = bf16[2048,2048]{1,0:T(8,128)(2,1)} async-done(((bf16[64,2048]{1,0:T(8,128)(2,1)}), bf16[2048,2048]{1,0:T(8,128)(2,1)}) %all-gather.5.cloned.1.call-update) | async-done | bytes 8388624 | tf_op jit(solution)/shard_map/all_gather | solution.py:100
  166.6 5.5 %convolution_convert_fusion = bf16[128,2048]{1,0:T(8,128)(2,1)} fusion(bf16[128,2048]{0,1:T(8,128)(2,1)S(1)} %bitcast.67, bf16[2048,2048]{1,0:T(8,128)(2,1)} %all-gather.5.cloned.1.call-done), kind=kOutput, calls=%fused_computation.3 | convolution fusion | flops 1074003968 | bytes 9437184 | tf_op jit(solution)/shard_map/dot_general | solution.py:98
  (62 shorter events, 12.1 us)
Async XLA Ops:
  6.5 15.5 %copy-start.2 = (bf16[128,2048]{1,0:T(8,128)(2,1)S(1)}, bf16[128,2048]{1,0:T(8,128)(2,1)}, u32[]{:S(2)}) copy-start(bf16[128,2048]{1,0:T(8,128)(2,1)} %param.9) | copy-start | bytes 1572868
  6.5 12.0 %all-to-all-start.2 = ((bf16[128,4,4]{0,2,1:T(4,128)(2,1)}), bf16[128,4,4]{0,2,1:T(4,128)(2,1)S(1)}, u32[]{:S(2)}, u32[]{:S(2)}) async-start(bf16[128,4,4]{0,2,1:T(4,128)(2,1)} %bitcast.83), calls=%async_computation.2 | async-start | bytes 8192 | tf_op jit(solution)/shard_map/all_to_all | solution.py:29
  18.6 16.8 %all-to-all-start.1 = ((bf16[128,4,512]{2,0,1:T(8,128)(2,1)}), bf16[128,4,512]{2,0,1:T(8,128)(2,1)S(1)}, u32[]{:S(2)}, u32[]{:S(2)}) async-start(bf16[128,4,512]{2,0,1:T(8,128)(2,1)} %bitcast.61), calls=%async_computation.1 | async-start | bytes 1048576 | tf_op jit(solution)/shard_map/all_to_all | solution.py:27
  35.3 17.3 %all-to-all-start.3 = ((bf16[128,4,512]{2,0,1:T(8,128)(2,1)}), bf16[128,4,512]{2,0,1:T(8,128)(2,1)S(1)}, u32[]{:S(2)}, u32[]{:S(2)}) async-start(bf16[128,4,512]{2,0,1:T(8,128)(2,1)} %bitcast.60), calls=%async_computation.3 | async-start | bytes 1048576 | tf_op jit(solution)/shard_map/all_to_all | solution.py:28
  38.8 45.7 %all-gather.7.cloned.1.call-start = ((), (), s32[]{:S(2)}) async-start(), calls=%async_computation.6 | async-start | bytes 2359296 | tf_op jit(solution)/shard_map/all_gather | solution.py:11
  52.7 5.4 %copy-start.3 = (bf16[128,2048]{1,0:T(8,128)(2,1)S(1)}, bf16[128,2048]{1,0:T(8,128)(2,1)}, u32[]{:S(2)}) copy-start(bf16[128,2048]{1,0:T(8,128)(2,1)} %param.7) | copy-start | bytes 1572868
  53.8 0.8 copy-start
  57.4 109.2 %all-gather.5.cloned.1.call-start = ((), (), s32[]{:S(2)}) async-start(), calls=%async_computation.5 | async-start | bytes 8650752 | tf_op jit(solution)/shard_map/all_gather | solution.py:100
  59.0 17.4 %all-to-all-start = ((bf16[128,4,512]{2,0,1:T(8,128)(2,1)}), bf16[128,4,512]{2,0,1:T(8,128)(2,1)S(1)}, u32[]{:S(2)}, u32[]{:S(2)}) async-start(bf16[128,4,512]{2,0,1:T(8,128)(2,1)} %bitcast.62), calls=%async_computation | async-start | bytes 1048576 | tf_op jit(solution)/shard_map/all_to_all | solution.py:26
  77.2 16.1 %copy-start.1 = (f32[2,4,128,128]{3,2,1,0:T(8,128)S(1)}, f32[2,4,128,128]{3,2,1,0:T(8,128)}, u32[]{:S(2)}) copy-start(f32[2,4,128,128]{3,2,1,0:T(8,128)} %copy-done) | copy-start | bytes 1572868
Sparse Core Ops, SparseCore 0:
  57.5 26.9 all-gather.6
  87.5 79.0 all-gather.4
where the time goes:
time: 180 us; the launch traced here: 179 us
  waiting for transfers between devices  80.3 us (45%)
  blocking collectives  33.1 us (18%)
  starting transfers between devices  16.9 us (9%)
  matrix products  15.2 us (8%)
  between operations  13.6 us (8%)
  other arithmetic  12.6 us (7%)
  local copies, waits for them, and re-layouts  6.89 us (4%)
    all_gather x1, waiting for transfers between devices, local(): lax.all_gather(out_weight, ('seq', 'head'), axis=0, tiled=True)  41.4 us
    all_to_all x1, blocking collectives, local(): lax.all_to_all(normed, 'head', split_axis=0, concat_axis=1, tiled=True)  24.3 us
    all_to_all x1, waiting for transfers between devices, local(): lax.all_to_all(values, 'head', split_axis=1, concat_axis=0, tiled=True)  13 us
    all_to_all x1, waiting for transfers between devices, local(): lax.all_to_all(keys, 'head', split_axis=1, concat_axis=0, tiled=True)  9.66 us
    all_gather x1, blocking collectives, entering(): everything = jax.tree.map(lambda part: lax.all_gather(part, axis), x)  8.76 us
    select_n x8, other arithmetic, turn(): return jax.tree.map(lambda a, b: jnp.where(reached, a, b), new, before)  8.42 us
    all_gather x1, waiting for transfers between devices, entering(): everything = jax.tree.map(lambda part: lax.all_gather(part, axis), x)  7.39 us
    all_to_all x1, starting transfers between devices, local(): lax.all_to_all(log_decay, 'head', split_axis=1, concat_axis=0, tiled=True)  6.45 us
  transfers between devices with their start and end apart: 6, of which 6 were waited for; matrix products, arithmetic and copies ran while one was open for 14% of the time, Pallas kernels for 0%

commit v1 on v0

v1 whole, which is shorter than its diff:
```python
import functools

import jax
import jax.numpy as jnp
from jax import lax
from jax.experimental import pallas as pl
from jax.experimental.pallas import tpu as pltpu
from jax.sharding import PartitionSpec as P

HD = 128
F32, BF16 = jnp.float32, jnp.bfloat16
MESH = pl.DeviceIdType.MESH


def contract(a, b, da, db):
    return lax.dot_general(a, b, (((da,), (db,)), ((), ())), preferred_element_type=F32)


def kernel(n_seq, n_head, heads, fused, *refs):
    if fused:
        q_ref, k_ref, v_ref, dec_ref, w_ref, o_ref = refs[:6]
        refs = refs[6:]
    else:
        q_ref, k_ref, v_ref, dec_ref, o_ref = refs[:5]
        refs = refs[5:]
    (st1, rc1, tb, rb, st3, rc3, pre, tot, inc, loc, s1s, s1r, s2s, s2r, s3s, s3r) = refs[:16]
    if fused:
        normed, wall, zup, zdn, zr, cxs, cxr, cys, cyr, ays, ayr, bxs, bxr, sbs, sbr = refs[16:]
    else:
        normed = o_ref
    rows = q_ref.shape[0]
    hg = heads // n_head
    span = hg * HD
    bits = n_seq.bit_length() - 1
    s, z = lax.axis_index("seq"), lax.axis_index("head")

    def flipped(k):
        bit = lax.rem(lax.div(s, 1 << k), 2)
        return s + (1 - 2 * bit) * (1 << k), bit

    def remote(src, dst, ssem, rsem, to):
        return pltpu.make_async_remote_copy(
            src_ref=src, dst_ref=dst, send_sem=ssem, recv_sem=rsem, device_id=to, device_id_type=MESH
        )

    barrier = pltpu.get_barrier_semaphore()
    for off in range(1, n_head):
        pl.semaphore_signal(barrier, inc=1, device_id=(s, lax.rem(z + off, n_head)), device_id_type=MESH)
    for k in range(bits):
        pl.semaphore_signal(barrier, inc=1, device_id=(flipped(k)[0], z), device_id_type=MESH)
    pl.semaphore_wait(barrier, n_head - 1 + bits)

    if fused:
        half = wall.shape[1]
        sib, sx, sy = (flipped(k)[0] for k in range(3))
        sxy = sx + sy - s

        def block(seq, zz):
            return wall.at[pl.ds(2 * (seq * n_head + zz), 2)]

        def part(seq, zz, which):
            return wall.at[2 * (seq * n_head + zz) + which]

        def up(zz):
            return remote(block(s, zz), block(s, zz), zup.at[zz], zr.at[zz], (s, z + 1))

        def down(zz):
            return remote(block(s, zz), block(s, zz), zdn.at[zz], zr.at[zz], (s, z - 1))

        def to_x(seq, zz):
            return remote(block(seq, zz), block(seq, zz), cxs.at[zz], cxr.at[zz], (sx, z))

        def to_y(seq, zz):
            return remote(block(seq, zz), block(seq, zz), cys.at[zz], cyr.at[zz], (sy, z))

        def a_to_y(seq, zz):
            return remote(part(seq, zz, 0), part(seq, zz, 0), ays.at[zz], ayr.at[zz], (sy, z))

        def b_to_x(seq, zz):
            return remote(part(seq, zz, 1), part(seq, zz, 1), bxs.at[zz], bxr.at[zz], (sx, z))

        def to_sib(kind, seq, zz):
            return remote(block(seq, zz), block(seq, zz), sbs.at[kind, zz], sbr.at[kind, zz], (sib, z))

        def near(j, body):
            if j == 0:
                body(z, 0)
                return
            pl.when(z - j >= 0)(lambda: body(z - j, 1))
            pl.when(z + j < n_head)(lambda: body(z + j, -1))

        def column(zz, way):
            if way:
                up(zz).wait_recv()
            if way >= 0:
                pl.when(z + 1 < n_head)(lambda: up(zz).start())
            if way <= 0:
                pl.when(z >= 1)(lambda: down(zz).start())
            to_x(s, zz).start()
            to_y(s, zz).start()
            to_sib(0, s, zz).start()

        def second(zz, way):
            to_x(sx, zz).wait_recv()
            a_to_y(sx, zz).start()
            to_sib(1, sx, zz).start()
            to_y(sy, zz).wait_recv()
            b_to_x(sy, zz).start()
            to_sib(2, sy, zz).start()

        def third(zz, way):
            a_to_y(sxy, zz).wait_recv()
            b_to_x(sxy, zz).wait_recv()
            to_sib(3, sxy, zz).start()

        mine = 2 * (s * n_head + z)
        wall[mine] = w_ref[:half]
        wall[mine + 1] = w_ref[half:]
        near(0, column)

    row_id = lax.broadcasted_iota(jnp.int32, (rows, rows), 0)
    col_id = lax.broadcasted_iota(jnp.int32, (rows, rows), 1)
    causal = row_id >= col_id
    dec = dec_ref[...]
    within = contract(causal.astype(F32).astype(BF16), dec, 1, 0)
    within_t = contract(dec, (row_id <= col_id).astype(F32).astype(BF16), 0, 0)
    key_scale = jnp.exp(within[rows - 1 : rows, :] - within)
    query_scale = jnp.exp(within)
    tile_row = lax.broadcasted_iota(jnp.int32, (16, HD), 0)

    def put_decays(ref, slot, decays):
        tile = jnp.zeros((16, HD), F32)
        for j, d in enumerate(decays):
            high = d.astype(BF16).astype(F32)
            tile = jnp.where(tile_row == 2 * j, high, tile)
            tile = jnp.where(tile_row == 2 * j + 1, d - high, tile)
        ref[slot, span : span + 16, :] = tile.astype(BF16)

    def get_decays(ref, slot):
        tile = ref[slot, span : span + 16, :].astype(F32)
        return [tile[2 * j : 2 * j + 1] + tile[2 * j + 1 : 2 * j + 2] for j in range(hg)]

    for g in range(n_head):
        decays = []
        for j in range(hg):
            h = g * hg + j
            at = slice(h * HD, (h + 1) * HD)
            scaled = (key_scale[:, h : h + 1] * k_ref[:, at].astype(F32)).astype(BF16)
            st1[g, j * HD : (j + 1) * HD, :] = contract(scaled, v_ref[:, at], 0, 0).astype(BF16)
            decays.append(jnp.broadcast_to(within_t[h : h + 1, rows - 1 : rows], (1, HD)))
        put_decays(st1, g, decays)

    def first(off):
        to = lax.rem(z + off, n_head)
        return remote(st1.at[to], rc1.at[z], s1s.at[off], s1r.at[z], (s, to))

    for off in range(1, n_head):
        first(off).start()
    rc1[z] = st1[z]

    def local(some):
        for h in some:
            at = slice(h * HD, (h + 1) * HD)
            gaps = within[:, h : h + 1] - within_t[h : h + 1, :]
            mask = jnp.exp(jnp.where(causal, gaps, -jnp.inf))
            weights = (contract(q_ref[:, at], k_ref[:, at], 1, 1) * mask).astype(BF16)
            loc[:, at] = contract(weights, v_ref[:, at], 1, 0)

    local(range(heads // 2))
    if fused:
        near(1, column)
    local(range(heads // 2, heads))
    if fused:
        near(2, column)
        near(0, second)

    for off in range(1, n_head):
        frm = lax.rem(z + off, n_head)
        remote(st1.at[frm], rc1.at[frm], s1s.at[off], s1r.at[frm], (s, frm)).wait_recv()
    arrived = [get_decays(rc1, zz) for zz in range(n_head)]
    before = [[jnp.zeros((1, HD), F32)] * hg]
    for zz in range(n_head):
        before.append([a + b for a, b in zip(before[-1], arrived[zz])])
    for j in range(hg):
        at = slice(j * HD, (j + 1) * HD)
        run = jnp.zeros((HD, HD), F32)
        for zz in range(n_head):
            pre[zz, at, :] = run
            run = jnp.exp(arrived[zz][j]) * run + rc1[zz, at, :].astype(F32)
        tot[at, :] = run
    inc[...] = jnp.zeros_like(inc)
    total = before[n_head]
    entering = [jnp.zeros((1, HD), F32)] * hg
    for k in range(bits):
        partner, bit = flipped(k)
        tb[k, :span, :] = tot[...].astype(BF16)
        put_decays(tb, k, total)
        swap = remote(tb.at[k], rb.at[k], s2s.at[k], s2r.at[k], (partner, z))
        swap.start()
        swap.wait_recv()
        theirs = get_decays(rb, k)
        later = jnp.broadcast_to(bit, (1, HD)) > 0
        for j in range(hg):
            at = slice(j * HD, (j + 1) * HD)
            other, own = rb[k, at, :].astype(F32), tot[at, :]
            take = jnp.where(later, jnp.exp(entering[j]), 0.0)
            inc[at, :] = inc[at, :] + take * other
            mine_scale = jnp.where(later, 1.0, jnp.exp(theirs[j]))
            other_scale = jnp.where(later, jnp.exp(total[j]), 1.0)
            tot[at, :] = mine_scale * own + other_scale * other
        entering = [jnp.where(later, a + b, a) for a, b in zip(entering, theirs)]
        total = [a + b for a, b in zip(total, theirs)]

    for zz in range(n_head):
        for j in range(hg):
            at = slice(j * HD, (j + 1) * HD)
            st3[zz, at, :] = (jnp.exp(before[zz][j]) * inc[at, :] + pre[zz, at, :]).astype(BF16)

    def last(off):
        to = lax.rem(z + off, n_head)
        return remote(st3.at[to], rc3.at[z], s3s.at[off], s3r.at[z], (s, to))

    for off in range(1, n_head):
        last(off).start()
    rc3[z] = st3[z]
    if fused:
        for j in range(3, n_head):
            near(j, column)
        for j in range(1, n_head):
            near(j, second)
        for j in range(n_head):
            near(j, third)

    for off in range(1, n_head):
        frm = lax.rem(z + off, n_head)
        remote(st3.at[frm], rc3.at[frm], s3s.at[off], s3r.at[frm], (s, frm)).wait_recv()
    for h in range(heads):
        at = slice(h * HD, (h + 1) * HD)
        j = h % hg
        scaled = (q_ref[:, at].astype(F32) * query_scale[:, h : h + 1]).astype(BF16)
        combined = loc[:, at] + contract(scaled, rc3[h // hg, j * HD : (j + 1) * HD, :], 1, 0)
        mean = jnp.mean(combined * combined, axis=-1, keepdims=True)
        normed[:, at] = (combined * lax.rsqrt(mean + 1e-05)).astype(BF16)

    if fused:
        for kind, flip in enumerate((sib, sib + sx - s, sib + sy - s, sib + sxy - s)):
            for zz in range(n_head):
                to_sib(kind, flip, zz).wait_recv()
        width = o_ref.shape[1]
        step = width // 4
        for c in range(0, width, step):
            w = wall[:, :, c : c + step].reshape(width, step)
            o_ref[:, c : c + step] = contract(normed[...], w, 1, 0).astype(BF16)
        for zz in range(n_head):
            pl.when((z >= zz) & (z + 1 < n_head))(lambda: up(zz).wait_send())
            pl.when((z <= zz) & (z >= 1))(lambda: down(zz).wait_send())
            to_x(s, zz).wait_send()
            to_y(s, zz).wait_send()
            a_to_y(sx, zz).wait_send()
            b_to_x(sy, zz).wait_send()
            for kind, seq in enumerate((s, sx, sy, sxy)):
                to_sib(kind, seq, zz).wait_send()
    for off in range(1, n_head):
        first(off).wait_send()
        last(off).wait_send()
    for k in range(bits):
        remote(tb.at[k], rb.at[k], s2s.at[k], s2r.at[k], (flipped(k)[0], z)).wait_send()


def local_part(queries, keys, values, log_decay, out_weight):
    n_seq, n_head = lax.axis_size("seq"), lax.axis_size("head")
    rows, width = queries.shape
    heads = log_decay.shape[1]
    bits = n_seq.bit_length() - 1
    span = heads // n_head * HD
    block = out_weight.shape[0]
    fused = n_seq == 8 and block % 32 == 0
    dma = pltpu.SemaphoreType.DMA
    scratch = [
        pltpu.VMEM((n_head, span + 16, HD), BF16),
        pltpu.VMEM((n_head, span + 16, HD), BF16),
        pltpu.VMEM((bits, span + 16, HD), BF16),
        pltpu.VMEM((bits, span + 16, HD), BF16),
        pltpu.VMEM((n_head, span, HD), BF16),
        pltpu.VMEM((n_head, span, HD), BF16),
        pltpu.VMEM((n_head, span, HD), F32),
        pltpu.VMEM((span, HD), F32),
        pltpu.VMEM((span, HD), F32),
        pltpu.VMEM((rows, width), F32),
        *(dma((n,)) for n in (n_head, n_head, bits, bits, n_head, n_head)),
    ]
    operands = [queries, keys, values, log_decay]
    if fused:
        operands.append(out_weight)
        scratch += [
            pltpu.VMEM((rows, width), BF16),
            pltpu.VMEM((2 * n_seq * n_head, block // 2, width), BF16),
            *(dma((n_head,)) for _ in range(11)),
            dma((4, n_head)),
            dma((4, n_head)),
        ]
    result = pl.pallas_call(
        functools.partial(kernel, n_seq, n_head, heads, fused),
        out_shape=jax.ShapeDtypeStruct((rows, width), BF16),
        in_specs=[pl.BlockSpec(memory_space=pltpu.VMEM)] * len(operands),
        out_specs=pl.BlockSpec(memory_space=pltpu.VMEM),
        scratch_shapes=scratch,
        compiler_params=pltpu.CompilerParams(
            collective_id=0, has_side_effects=True, vmem_limit_bytes=40 * 1024 * 1024
        ),
    )(*operands)
    if fused:
        return result
    weight = lax.all_gather(out_weight, ("seq", "head"), axis=0, tiled=True)
    return jnp.dot(result, weight, preferred_element_type=F32).astype(BF16)


def solution(mesh):
    placed = P(("seq", "head"), None)
    return jax.shard_map(
        local_part, mesh=mesh, in_specs=(placed,) * 5, out_specs=placed, check_vma=False
    )
```

time: 180 us -> 67.9 us (0.38)
  waiting for transfers between devices: 80.3 us -> 0 us
  Pallas kernels: 0 us -> 61.9 us
  blocking collectives: 33.1 us -> 0 us
  starting transfers between devices: 16.9 us -> 0 us
  matrix products: 15.2 us -> 0 us
  between operations: 13.6 us -> 0.02 us
  other arithmetic: 12.6 us -> 0 us
    pallas_call x0 -> x1, Pallas kernels: none -> 61.9 us  [local_part(): pl.pallas_call(functools.partial(kernel, n_seq, n_head, heads, fused), ou...]
    all_gather x2 -> x0, waiting for transfers between devices: 48.8 us -> none  [the longest x1 41.4 us: local(): lax.all_gather(out_weight, ('seq', 'head'), axis=0, tiled=True)]
    all_to_all x4 -> x0, waiting for transfers between devices: 30.8 us -> none  [the longest x1 13 us: local(): lax.all_to_all(values, 'head', split_axis=1, concat_axis=0, tiled=True)]
    all_to_all x1 -> x0, blocking collectives: 24.3 us -> none  [local(): lax.all_to_all(normed, 'head', split_axis=0, concat_axis=1, tiled=True)]
    all_to_all x4 -> x0, starting transfers between devices: 16.9 us -> none  [the longest x1 6.45 us: local(): lax.all_to_all(log_decay, 'head', split_axis=1, concat_axis=0, tiled=True)]
    dot_general x6 -> x0, matrix products: 15.2 us -> none  [the longest x1 5.46 us: local(): jnp.dot(restored, lax.all_gather(out_weight, ('seq', 'head'), axis=0, til...]
    all_gather x1 -> x0, blocking collectives: 8.76 us -> none  [entering(): everything = jax.tree.map(lambda part: lax.all_gather(part, axis), x)]
    select_n x8 -> x0, other arithmetic: 8.42 us -> none  [turn(): return jax.tree.map(lambda a, b: jnp.where(reached, a, b), new, before)]
  transfers between devices with their start and end apart: 6 -> 0, of which waited for: 6 -> 0; matrix products, arithmetic and copies ran while one was open for 14% -> 0% of each run, Pallas kernels for 0% -> 0%
where the time goes in v1:
time: 67.9 us; the launch traced here: 67.6 us
  Pallas kernels  61.9 us (91%)
  local copies, waits for them, and re-layouts  5.67 us (8%)
    pallas_call x1, Pallas kernels, local_part(): pl.pallas_call(functools.partial(kernel, n_seq, n_head, heads, fused), ou...  61.9 us
    unnamed x10, local copies, waits for them, and re-layouts  5.67 us

profile of v1, /device:TPU:0, one launch (start us, length us, event | category | flops | bytes accessed | tf_op | source)
XLA Modules:
  0.0 67.6 jit_solution(4255017981089205972)
XLA Ops:
  0.0 0.8 %copy.6.refs_3_ = bf16[128,16]{1,0:T(8,128)(2,1)S(1)} copy(bf16[128,16]{0,1:T(8,128)(2,1)} %param.8) | data formatting | bytes 8192 | tf_op args[3]
  0.8 0.0 copy-start
  0.8 1.0 %copy-done = bf16[128,2048]{1,0:T(8,128)(2,1)S(1)} copy-done((bf16[128,2048]{1,0:T(8,128)(2,1)S(1)}, bf16[128,2048]{1,0:T(8,128)(2,1)}, u32[]{:S(2)}) %copy-start) | copy-done | bytes 524312
  1.8 0.0 copy-start.1
  1.9 1.0 %copy-done.1 = bf16[128,2048]{1,0:T(8,128)(2,1)S(1)} copy-done((bf16[128,2048]{1,0:T(8,128)(2,1)S(1)}, bf16[128,2048]{1,0:T(8,128)(2,1)}, u32[]{:S(2)}) %copy-start.1) | copy-done | bytes 524312
  2.9 0.0 copy-start.2
  2.9 1.0 %copy-done.2 = bf16[128,2048]{1,0:T(8,128)(2,1)S(1)} copy-done((bf16[128,2048]{1,0:T(8,128)(2,1)S(1)}, bf16[128,2048]{1,0:T(8,128)(2,1)}, u32[]{:S(2)}) %copy-start.2) | copy-done | bytes 524312
  3.9 0.0 copy-start.3
  3.9 0.9 %copy-done.3 = bf16[64,2048]{1,0:T(8,128)(2,1)S(1)} copy-done((bf16[64,2048]{1,0:T(8,128)(2,1)S(1)}, bf16[64,2048]{1,0:T(8,128)(2,1)}, u32[]{:S(2)}) %copy-start.3) | copy-done | bytes 262168
  4.9 61.9 %shard_map.55 = bf16[128,2048]{1,0:T(8,128)(2,1)S(1)} custom-call(bf16[128,2048]{1,0:T(8,128)(2,1)S(1)} %copy-done, bf16[128,2048]{1,0:T(8,128)(2,1)S(1)} %copy-done.1, bf16[128,2048]{1,0:T(8,128)(2,1)S(1)} %copy-done.2, bf16[128,16]{1,0:T(8,128)(2,1)S(1)} %copy.6.refs_3_, bf16[64,2048]{1,0:T(8,128)(2,1)S(1)} %copy-done.3), custom_call_target="tpu_custom_call" | custom-call | tf_op jit(solution)/shard_map/pallas_call | solution.py:302
  66.8 0.8 %copy.8 = bf16[128,2048]{1,0:T(8,128)(2,1)} copy(bf16[128,2048]{1,0:T(8,128)(2,1)S(1)} %shard_map.55) | data formatting | bytes 1048576
Async XLA Ops:
  0.8 1.0 %copy-start = (bf16[128,2048]{1,0:T(8,128)(2,1)S(1)}, bf16[128,2048]{1,0:T(8,128)(2,1)}, u32[]{:S(2)}) copy-start(bf16[128,2048]{1,0:T(8,128)(2,1)} %refs_0_.1) | copy-start | bytes 1572868
  1.8 1.0 %copy-start.1 = (bf16[128,2048]{1,0:T(8,128)(2,1)S(1)}, bf16[128,2048]{1,0:T(8,128)(2,1)}, u32[]{:S(2)}) copy-start(bf16[128,2048]{1,0:T(8,128)(2,1)} %refs_1_.1) | copy-start | bytes 1572868
  2.9 1.0 %copy-start.2 = (bf16[128,2048]{1,0:T(8,128)(2,1)S(1)}, bf16[128,2048]{1,0:T(8,128)(2,1)}, u32[]{:S(2)}) copy-start(bf16[128,2048]{1,0:T(8,128)(2,1)} %refs_2_.1) | copy-start | bytes 1572868
  3.9 0.9 %copy-start.3 = (bf16[64,2048]{1,0:T(8,128)(2,1)S(1)}, bf16[64,2048]{1,0:T(8,128)(2,1)}, u32[]{:S(2)}) copy-start(bf16[64,2048]{1,0:T(8,128)(2,1)} %refs_4_.1) | copy-start | bytes 786436

commit v2 on v1

v2 whole, which is shorter than its diff:
```python
import functools

import jax
import jax.numpy as jnp
from jax import lax
from jax.experimental import pallas as pl
from jax.experimental.pallas import tpu as pltpu
from jax.sharding import PartitionSpec as P

HD = 128
F32, BF16 = jnp.float32, jnp.bfloat16
MESH = pl.DeviceIdType.MESH


def contract(a, b, da, db):
    return lax.dot_general(a, b, (((da,), (db,)), ((), ())), preferred_element_type=F32)


def kernel(n_seq, n_head, heads, fused, *refs):
    if fused:
        q_hbm, k_hbm, v_hbm, dec_hbm, w_hbm, o_ref = refs[:6]
        refs = refs[6:]
    else:
        q_hbm, k_hbm, v_hbm, dec_hbm, o_ref = refs[:5]
        refs = refs[5:]
    (q_ref, k_ref, v_ref, dec_ref, lds, st1, rc1, tb, rb, st3, rc3, pre, tot, inc, loc) = refs[:15]
    s1s, s1r, s2s, s2r, s3s, s3r = refs[15:21]
    if fused:
        normed, wall, zup, zdn, zr, cxs, cxr, cys, cyr, ays, ayr, bxs, bxr, sbs, sbr = refs[21:]
    else:
        normed = o_ref
    rows = q_ref.shape[0]
    batches = st1.shape[0]
    hg = heads // n_head // batches
    span = hg * HD
    bits = n_seq.bit_length() - 1
    s, z = lax.axis_index("seq"), lax.axis_index("head")

    def flipped(k):
        bit = lax.rem(lax.div(s, 1 << k), 2)
        return s + (1 - 2 * bit) * (1 << k), bit

    def remote(src, dst, ssem, rsem, to):
        return pltpu.make_async_remote_copy(
            src_ref=src, dst_ref=dst, send_sem=ssem, recv_sem=rsem, device_id=to, device_id_type=MESH
        )

    loads = [
        pltpu.make_async_copy(src, dst, lds.at[i])
        for i, (src, dst) in enumerate(((dec_hbm, dec_ref), (k_hbm, k_ref), (v_hbm, v_ref), (q_hbm, q_ref)))
    ]
    if fused:
        half = wall.shape[1]
        mine = 2 * (s * n_head + z)
        own = [
            pltpu.make_async_copy(w_hbm.at[pl.ds(i * half, half)], wall.at[mine + i], lds.at[4 + i])
            for i in range(2)
        ]
        for copy in own:
            copy.start()
    for copy in loads:
        copy.start()

    barrier = pltpu.get_barrier_semaphore()
    for off in range(1, n_head):
        pl.semaphore_signal(barrier, inc=1, device_id=(s, lax.rem(z + off, n_head)), device_id_type=MESH)
    for k in range(bits):
        pl.semaphore_signal(barrier, inc=1, device_id=(flipped(k)[0], z), device_id_type=MESH)
    pl.semaphore_wait(barrier, n_head - 1 + bits)

    if fused:
        sib, sx, sy = (flipped(k)[0] for k in range(3))
        sxy = sx + sy - s

        def block(seq, zz):
            return wall.at[pl.ds(2 * (seq * n_head + zz), 2)]

        def part(seq, zz, which):
            return wall.at[2 * (seq * n_head + zz) + which]

        def up(zz):
            return remote(block(s, zz), block(s, zz), zup.at[zz], zr.at[zz], (s, z + 1))

        def down(zz):
            return remote(block(s, zz), block(s, zz), zdn.at[zz], zr.at[zz], (s, z - 1))

        def to_x(seq, zz):
            return remote(block(seq, zz), block(seq, zz), cxs.at[zz], cxr.at[zz], (sx, z))

        def to_y(seq, zz):
            return remote(block(seq, zz), block(seq, zz), cys.at[zz], cyr.at[zz], (sy, z))

        def a_to_y(seq, zz):
            return remote(part(seq, zz, 0), part(seq, zz, 0), ays.at[zz], ayr.at[zz], (sy, z))

        def b_to_x(seq, zz):
            return remote(part(seq, zz, 1), part(seq, zz, 1), bxs.at[zz], bxr.at[zz], (sx, z))

        def to_sib(kind, seq, zz):
            return remote(block(seq, zz), block(seq, zz), sbs.at[kind, zz], sbr.at[kind, zz], (sib, z))

        def near(j, body):
            if j == 0:
                body(z, 0)
                return
            pl.when(z - j >= 0)(lambda: body(z - j, 1))
            pl.when(z + j < n_head)(lambda: body(z + j, -1))

        def column(zz, way):
            if way:
                up(zz).wait_recv()
            if way >= 0:
                pl.when(z + 1 < n_head)(lambda: up(zz).start())
            if way <= 0:
                pl.when(z >= 1)(lambda: down(zz).start())
            to_x(s, zz).start()
            to_y(s, zz).start()
            to_sib(0, s, zz).start()

        def second(zz, way):
            to_x(sx, zz).wait_recv()
            a_to_y(sx, zz).start()
            to_sib(1, sx, zz).start()
            to_y(sy, zz).wait_recv()
            b_to_x(sy, zz).start()
            to_sib(2, sy, zz).start()

        def third(zz, way):
            a_to_y(sxy, zz).wait_recv()
            b_to_x(sxy, zz).wait_recv()
            to_sib(3, sxy, zz).start()

        for copy in own:
            copy.wait()
        near(0, column)

    row_id = lax.broadcasted_iota(jnp.int32, (rows, rows), 0)
    col_id = lax.broadcasted_iota(jnp.int32, (rows, rows), 1)
    causal = row_id >= col_id
    loads[0].wait()
    dec = dec_ref[...]
    within = contract(causal.astype(F32).astype(BF16), dec, 1, 1)
    within_t = contract(dec, (row_id <= col_id).astype(F32).astype(BF16), 1, 0)
    key_scale = jnp.exp(within[rows - 1 : rows, :] - within)
    query_scale = jnp.exp(within)
    tile_row = lax.broadcasted_iota(jnp.int32, (16, HD), 0)

    def put_decays(ref, where, decays):
        tile = jnp.zeros((16, HD), F32)
        for j, d in enumerate(decays):
            high = d.astype(BF16).astype(F32)
            tile = jnp.where(tile_row == 2 * j, high, tile)
            tile = jnp.where(tile_row == 2 * j + 1, d - high, tile)
        ref[(*where, slice(span, span + 16), slice(None))] = tile.astype(BF16)

    def get_decays(ref, where):
        tile = ref[(*where, slice(span, span + 16), slice(None))].astype(F32)
        return [tile[2 * j : 2 * j + 1] + tile[2 * j + 1 : 2 * j + 2] for j in range(hg)]

    def head_of(b, g, j):
        return (g * batches + b) * hg + j

    def columns(h):
        return slice(h * HD, (h + 1) * HD)

    def state_rows(j):
        return slice(j * HD, (j + 1) * HD)

    def first(b, to, frm, off):
        return remote(st1.at[b, to], rc1.at[b, frm], s1s.at[b, off], s1r.at[b, frm], (s, to))

    def swap(b, k):
        return remote(tb.at[b, k], rb.at[b, k], s2s.at[b, k], s2r.at[b, k], (flipped(k)[0], z))

    def last(b, to, frm, off):
        return remote(st3.at[b, to], rc3.at[b, frm], s3s.at[b, off], s3r.at[b, frm], (s, to))

    def around(body):
        for off in range(1, n_head):
            body(lax.rem(z + off, n_head), off)

    def block_states(b):
        for g in range(n_head):
            decays = []
            for j in range(hg):
                h = head_of(b, g, j)
                scaled = (key_scale[:, h : h + 1] * k_ref[:, columns(h)].astype(F32)).astype(BF16)
                st1[b, g, state_rows(j), :] = contract(scaled, v_ref[:, columns(h)], 0, 0).astype(BF16)
                decays.append(jnp.broadcast_to(within_t[h : h + 1, rows - 1 : rows], (1, HD)))
            put_decays(st1, (b, g), decays)
        around(lambda to, off: first(b, to, z, off).start())
        rc1[b, z] = st1[b, z]

    def local(some):
        for h in some:
            at = columns(h)
            gaps = within[:, h : h + 1] - within_t[h : h + 1, :]
            mask = jnp.exp(jnp.where(causal, gaps, -jnp.inf))
            weights = (contract(q_ref[:, at], k_ref[:, at], 1, 1) * mask).astype(BF16)
            loc[:, at] = contract(weights, v_ref[:, at], 1, 0)

    before, total, entering = {}, {}, {}

    def send_total(b, k):
        tb[b, k, :span, :] = tot[b].astype(BF16)
        put_decays(tb, (b, k), total[b])
        swap(b, k).start()

    def over_head(b):
        around(lambda frm, off: first(b, frm, frm, off).wait_recv())
        arrived = [get_decays(rc1, (b, zz)) for zz in range(n_head)]
        sums = [[jnp.zeros((1, HD), F32)] * hg]
        for zz in range(n_head):
            sums.append([x + y for x, y in zip(sums[-1], arrived[zz])])
        for j in range(hg):
            at = state_rows(j)
            run = jnp.zeros((HD, HD), F32)
            for zz in range(n_head):
                pre[b, zz, at, :] = run
                run = jnp.exp(arrived[zz][j]) * run + rc1[b, zz, at, :].astype(F32)
            tot[b, at, :] = run
            inc[b, at, :] = jnp.zeros((HD, HD), F32)
        before[b], total[b], entering[b] = sums, sums[n_head], [jnp.zeros((1, HD), F32)] * hg
        send_total(b, 0)

    def over_seq(b, k):
        swap(b, k).wait_recv()
        later = jnp.broadcast_to(flipped(k)[1], (1, HD)) > 0
        theirs = get_decays(rb, (b, k))
        for j in range(hg):
            at = state_rows(j)
            other, ours = rb[b, k, at, :].astype(F32), tot[b, at, :]
            take = jnp.where(later, jnp.exp(entering[b][j]), 0.0)
            inc[b, at, :] = inc[b, at, :] + take * other
            ours_scale = jnp.where(later, 1.0, jnp.exp(theirs[j]))
            other_scale = jnp.where(later, jnp.exp(total[b][j]), 1.0)
            tot[b, at, :] = ours_scale * ours + other_scale * other
        entering[b] = [jnp.where(later, x + y, x) for x, y in zip(entering[b], theirs)]
        total[b] = [x + y for x, y in zip(total[b], theirs)]
        if k + 1 < bits:
            send_total(b, k + 1)
            return
        for zz in range(n_head):
            for j in range(hg):
                at = state_rows(j)
                st3[b, zz, at, :] = (jnp.exp(before[b][zz][j]) * inc[b, at, :] + pre[b, zz, at, :]).astype(BF16)
        around(lambda to, off: last(b, to, z, off).start())
        rc3[b, z] = st3[b, z]

    def finish(b):
        around(lambda frm, off: last(b, frm, frm, off).wait_recv())
        for g in range(n_head):
            for j in range(hg):
                h = head_of(b, g, j)
                at = columns(h)
                carried = contract(q_ref[:, at], rc3[b, g, state_rows(j), :], 1, 0)
                combined = loc[:, at] + query_scale[:, h : h + 1] * carried
                mean = jnp.mean(combined * combined, axis=-1, keepdims=True)
                normed[:, at] = (combined * lax.rsqrt(mean + 1e-05)).astype(BF16)

    relays = []
    if fused:
        relays = [(1, column), (0, second), (2, column), (1, second), (3, column), (2, second), (3, second)]
        relays += [(j, third) for j in range(n_head)]

    def relay(count=1):
        for _ in range(count):
            if relays:
                near(*relays.pop(0))

    loads[1].wait()
    loads[2].wait()
    for b in range(batches):
        block_states(b)
    loads[3].wait()
    local(range(heads // 2))
    relay()
    local(range(heads // 2, heads))
    for b in range(batches):
        over_head(b)
    for k in range(bits):
        for b in range(batches):
            relay()
            over_seq(b, k)
    relay(len(relays))
    for b in range(batches):
        finish(b)

    if fused:
        for kind, flip in enumerate((sib, sib + sx - s, sib + sy - s, sib + sxy - s)):
            for zz in range(n_head):
                to_sib(kind, flip, zz).wait_recv()
        width = o_ref.shape[1]
        step = width // 4
        for c in range(0, width, step):
            w = wall[:, :, c : c + step].reshape(width, step)
            o_ref[:, c : c + step] = contract(normed[...], w, 1, 0).astype(BF16)
        for zz in range(n_head):
            pl.when((z >= zz) & (z + 1 < n_head))(lambda: up(zz).wait_send())
            pl.when((z <= zz) & (z >= 1))(lambda: down(zz).wait_send())
            to_x(s, zz).wait_send()
            to_y(s, zz).wait_send()
            a_to_y(sx, zz).wait_send()
            b_to_x(sy, zz).wait_send()
            for kind, seq in enumerate((s, sx, sy, sxy)):
                to_sib(kind, seq, zz).wait_send()
    for b in range(batches):
        around(lambda to, off: first(b, to, z, off).wait_send())
        for k in range(bits):
            swap(b, k).wait_send()
        around(lambda to, off: last(b, to, z, off).wait_send())


def local_part(queries, keys, values, log_decay, out_weight):
    n_seq, n_head = lax.axis_size("seq"), lax.axis_size("head")
    rows, width = queries.shape
    heads = log_decay.shape[1]
    bits = n_seq.bit_length() - 1
    batches = 2 if heads // n_head % 2 == 0 else 1
    span = heads // n_head // batches * HD
    block = out_weight.shape[0]
    fused = n_seq == 8 and block % 32 == 0
    dma = pltpu.SemaphoreType.DMA
    scratch = [
        *(pltpu.VMEM((rows, width), BF16) for _ in range(3)),
        pltpu.VMEM((heads, rows), BF16),
        dma((6,)),
        pltpu.VMEM((batches, n_head, span + 16, HD), BF16),
        pltpu.VMEM((batches, n_head, span + 16, HD), BF16),
        pltpu.VMEM((batches, bits, span + 16, HD), BF16),
        pltpu.VMEM((batches, bits, span + 16, HD), BF16),
        pltpu.VMEM((batches, n_head, span, HD), BF16),
        pltpu.VMEM((batches, n_head, span, HD), BF16),
        pltpu.VMEM((batches, n_head, span, HD), F32),
        pltpu.VMEM((batches, span, HD), F32),
        pltpu.VMEM((batches, span, HD), F32),
        pltpu.VMEM((rows, width), F32),
        *(dma((batches, n)) for n in (n_head, n_head, bits, bits, n_head, n_head)),
    ]
    operands = [queries, keys, values, log_decay.T]
    if fused:
        operands.append(out_weight)
        scratch += [
            pltpu.VMEM((rows, width), BF16),
            pltpu.VMEM((2 * n_seq * n_head, block // 2, width), BF16),
            *(dma((n_head,)) for _ in range(11)),
            dma((4, n_head)),
            dma((4, n_head)),
        ]
    result = pl.pallas_call(
        functools.partial(kernel, n_seq, n_head, heads, fused),
        out_shape=jax.ShapeDtypeStruct((rows, width), BF16),
        in_specs=[pl.BlockSpec(memory_space=pltpu.HBM)] * len(operands),
        out_specs=pl.BlockSpec(memory_space=pltpu.VMEM),
        scratch_shapes=scratch,
        compiler_params=pltpu.CompilerParams(
            collective_id=0, has_side_effects=True, vmem_limit_bytes=40 * 1024 * 1024
        ),
    )(*operands)
    if fused:
        return result
    weight = lax.all_gather(out_weight, ("seq", "head"), axis=0, tiled=True)
    return jnp.dot(result, weight, preferred_element_type=F32).astype(BF16)


def solution(mesh):
    placed = P(("seq", "head"), None)
    return jax.shard_map(
        local_part, mesh=mesh, in_specs=(placed,) * 5, out_specs=placed, check_vma=False
    )
```

time: 67.9 us -> 61.7 us (0.909)
  Pallas kernels: 61.9 us -> 55.8 us
    pallas_call x1, Pallas kernels: 61.9 us -> 55.8 us  [local_part(): pl.pallas_call(functools.partial(kernel, n_seq, n_head, heads, fused), ou...]
    unnamed x10 -> x11, local copies, waits for them, and re-layouts: 5.67 us -> 5.55 us
where the time goes in v2:
time: 61.7 us; the launch traced here: 61.4 us
  Pallas kernels  55.8 us (90%)
  local copies, waits for them, and re-layouts  5.55 us (9%)
    pallas_call x1, Pallas kernels, local_part(): pl.pallas_call(functools.partial(kernel, n_seq, n_head, heads, fused), ou...  55.8 us
    unnamed x11, local copies, waits for them, and re-layouts  5.55 us

profile of v2, /device:TPU:0, one launch (start us, length us, event | category | flops | bytes accessed | tf_op | source)
XLA Modules:
  0.0 61.4 jit_solution(2017684592574166211)
XLA Ops:
  0.0 0.0 copy-start
  0.0 1.0 %copy-done = bf16[128,2048]{1,0:T(8,128)(2,1)S(1)} copy-done((bf16[128,2048]{1,0:T(8,128)(2,1)S(1)}, bf16[128,2048]{1,0:T(8,128)(2,1)}, u32[]{:S(2)}) %copy-start) | copy-done | bytes 524312
  1.0 0.0 copy-start.1
  1.0 1.0 %copy-done.1 = bf16[128,2048]{1,0:T(8,128)(2,1)S(1)} copy-done((bf16[128,2048]{1,0:T(8,128)(2,1)S(1)}, bf16[128,2048]{1,0:T(8,128)(2,1)}, u32[]{:S(2)}) %copy-start.1) | copy-done | bytes 524312
  2.1 0.0 copy-start.2
  2.1 1.0 %copy-done.2 = bf16[128,2048]{1,0:T(8,128)(2,1)S(1)} copy-done((bf16[128,2048]{1,0:T(8,128)(2,1)S(1)}, bf16[128,2048]{1,0:T(8,128)(2,1)}, u32[]{:S(2)}) %copy-start.2) | copy-done | bytes 524312
  3.1 0.0 copy-start.3
  3.1 0.9 %copy-done.3 = bf16[64,2048]{1,0:T(8,128)(2,1)S(1)} copy-done((bf16[64,2048]{1,0:T(8,128)(2,1)S(1)}, bf16[64,2048]{1,0:T(8,128)(2,1)}, u32[]{:S(2)}) %copy-start.3) | copy-done | bytes 262168
  4.1 0.0 copy-start.4
  4.1 0.7 %copy-done.4 = bf16[128,16]{0,1:T(8,128)(2,1)S(1)} copy-done((bf16[128,16]{0,1:T(8,128)(2,1)S(1)}, bf16[128,16]{0,1:T(8,128)(2,1)}, u32[]{:S(2)}) %copy-start.4) | copy-done | bytes 4120
  4.8 55.8 %shard_map.55 = bf16[128,2048]{1,0:T(8,128)(2,1)S(1)} custom-call(bf16[128,2048]{1,0:T(8,128)(2,1)S(1)} %copy-done, bf16[128,2048]{1,0:T(8,128)(2,1)S(1)} %copy-done.1, bf16[128,2048]{1,0:T(8,128)(2,1)S(1)} %copy-done.2, bf16[16,128]{1,0:T(8,128)(2,1)S(1)} %bitcast.1, bf16[64,2048]{1,0:T(8,128)(2,1)S(1)} %copy-done.3), custom_call_target="tpu_custom_call" | custom-call | tf_op jit(solution)/shard_map/pallas_call | solution.py:350
  60.6 0.8 %copy.7 = bf16[128,2048]{1,0:T(8,128)(2,1)} copy(bf16[128,2048]{1,0:T(8,128)(2,1)S(1)} %shard_map.55) | data formatting | bytes 1048576
Async XLA Ops:
  0.0 1.0 %copy-start = (bf16[128,2048]{1,0:T(8,128)(2,1)S(1)}, bf16[128,2048]{1,0:T(8,128)(2,1)}, u32[]{:S(2)}) copy-start(bf16[128,2048]{1,0:T(8,128)(2,1)} %refs_0_.1) | copy-start | bytes 1572868
  1.0 1.0 %copy-start.1 = (bf16[128,2048]{1,0:T(8,128)(2,1)S(1)}, bf16[128,2048]{1,0:T(8,128)(2,1)}, u32[]{:S(2)}) copy-start(bf16[128,2048]{1,0:T(8,128)(2,1)} %refs_1_.1) | copy-start | bytes 1572868
  2.1 1.0 %copy-start.2 = (bf16[128,2048]{1,0:T(8,128)(2,1)S(1)}, bf16[128,2048]{1,0:T(8,128)(2,1)}, u32[]{:S(2)}) copy-start(bf16[128,2048]{1,0:T(8,128)(2,1)} %refs_2_.1) | copy-start | bytes 1572868
  3.1 0.9 %copy-start.3 = (bf16[64,2048]{1,0:T(8,128)(2,1)S(1)}, bf16[64,2048]{1,0:T(8,128)(2,1)}, u32[]{:S(2)}) copy-start(bf16[64,2048]{1,0:T(8,128)(2,1)} %refs_4_.1) | copy-start | bytes 786436
  4.1 0.7 %copy-start.4 = (bf16[128,16]{0,1:T(8,128)(2,1)S(1)}, bf16[128,16]{0,1:T(8,128)(2,1)}, u32[]{:S(2)}) copy-start(bf16[128,16]{0,1:T(8,128)(2,1)} %param.8) | copy-start | bytes 12292

commit v3 on v2

--- a/solution.py
+++ b/solution.py
@@ -10,6 +10,11 @@
 HD = 128
 F32, BF16 = jnp.float32, jnp.bfloat16
 MESH = pl.DeviceIdType.MESH
+ORDER = (
+    "L0", "L1", "X0", "H0", "C2", "H1", "S00", "S01", "X1", "S10",
+    "S11", "C3", "S20", "S21", "X2", "X3", "T0", "T1", "T2", "F0",
+    "F1", "P0", "P1", "T3", "P2", "P3", "P4", "P5", "P6", "P7",
+)
 
 
 def contract(a, b, da, db):
@@ -258,43 +263,55 @@
                 mean = jnp.mean(combined * combined, axis=-1, keepdims=True)
                 normed[:, at] = (combined * lax.rsqrt(mean + 1e-05)).astype(BF16)
 
-    relays = []
-    if fused:
-        relays = [(1, column), (0, second), (2, column), (1, second), (3, column), (2, second), (3, second)]
-        relays += [(j, third) for j in range(n_head)]
-
-    def relay(count=1):
-        for _ in range(count):
-            if relays:
-                near(*relays.pop(0))
+    def project(n):
+        far, kind = n % 2, n // 2
+        seq = (s, sx, sy, sxy)[kind]
+        if far:
+            seq = seq + sib - s
+            for zz in range(n_head):
+                to_sib(kind, seq, zz).wait_recv()
+        width = o_ref.shape[1]
+        deep = 2 * n_head * half
+        left = normed[:, pl.ds(pl.multiple_of(seq * deep, deep), deep)]
+        for c in range(0, width, width // 4):
+            at = slice(c, c + width // 4)
+            right = wall[pl.ds(seq * 2 * n_head, 2 * n_head), :, at].reshape(deep, width // 4)
+            piece = contract(left, right, 1, 0)
+            if n == 0:
+                loc[:, at] = piece
+            elif n < 7:
+                loc[:, at] = loc[:, at] + piece
+            else:
+                o_ref[:, at] = (loc[:, at] + piece).astype(BF16)
+
+    def run_step(step):
+        kind, n = step[0], int(step[1:])
+        if kind in "CXT":
+            if fused:
+                near(n, {"C": column, "X": second, "T": third}[kind]) if n < n_head else None
+        elif kind == "P":
+            project(n)
+        elif kind == "L":
+            local(range(n * heads // 2, (n + 1) * heads // 2))
+        elif kind == "S":
+            if n % 10 < batches:
+                over_seq(n % 10, n // 10)
+        elif n < batches:
+            {"H": over_head, "F": finish}[kind](n)
 
     loads[1].wait()
     loads[2].wait()
-    for b in range(batches):
+    block_states(0)
+    if fused:
+        near(1, column)
+    for b in range(1, batches):
         block_states(b)
     loads[3].wait()
-    local(range(heads // 2))
-    relay()
-    local(range(heads // 2, heads))
-    for b in range(batches):
-        over_head(b)
-    for k in range(bits):
-        for b in range(batches):
-            relay()
-            over_seq(b, k)
-    relay(len(relays))
-    for b in range(batches):
-        finish(b)
-
-    if fused:
-        for kind, flip in enumerate((sib, sib + sx - s, sib + sy - s, sib + sxy - s)):
-            for zz in range(n_head):
-                to_sib(kind, flip, zz).wait_recv()
-        width = o_ref.shape[1]
-        step = width // 4
-        for c in range(0, width, step):
-            w = wall[:, :, c : c + step].reshape(width, step)
-            o_ref[:, c : c + step] = contract(normed[...], w, 1, 0).astype(BF16)
+    order = ORDER if fused else ["L0", "L1", "H0", "H1", *(f"S{k}{b}" for k in range(bits) for b in range(batches)), "F0", "F1"]
+    for step in order:
+        run_step(step)
+
+    if fused:
         for zz in range(n_head):
             pl.when((z >= zz) & (z + 1 < n_head))(lambda: up(zz).wait_send())
             pl.when((z <= zz) & (z >= 1))(lambda: down(zz).wait_send())

time: 61.7 us -> 60.1 us (0.974)
  Pallas kernels: 55.8 us -> 54.1 us
    pallas_call x1, Pallas kernels: 55.8 us -> 54.1 us  [local_part(): pl.pallas_call(functools.partial(kernel, n_seq, n_head, heads, fused), ou...]
where the time goes in v3:
time: 60.1 us; the launch traced here: 59.7 us
  Pallas kernels  54.1 us (90%)
  local copies, waits for them, and re-layouts  5.55 us (9%)
    pallas_call x1, Pallas kernels, local_part(): pl.pallas_call(functools.partial(kernel, n_seq, n_head, heads, fused), ou...  54.1 us
    unnamed x11, local copies, waits for them, and re-layouts  5.55 us

profile of v3, /device:TPU:0, one launch (start us, length us, event | category | flops | bytes accessed | tf_op | source)
XLA Modules:
  0.0 59.7 jit_solution(709992841531096243)
XLA Ops:
  0.0 0.0 copy-start
  0.0 1.0 %copy-done = bf16[128,2048]{1,0:T(8,128)(2,1)S(1)} copy-done((bf16[128,2048]{1,0:T(8,128)(2,1)S(1)}, bf16[128,2048]{1,0:T(8,128)(2,1)}, u32[]{:S(2)}) %copy-start) | copy-done | bytes 524312
  1.0 0.0 copy-start.1
  1.0 1.0 %copy-done.1 = bf16[128,2048]{1,0:T(8,128)(2,1)S(1)} copy-done((bf16[128,2048]{1,0:T(8,128)(2,1)S(1)}, bf16[128,2048]{1,0:T(8,128)(2,1)}, u32[]{:S(2)}) %copy-start.1) | copy-done | bytes 524312
  2.1 0.0 copy-start.2
  2.1 1.0 %copy-done.2 = bf16[128,2048]{1,0:T(8,128)(2,1)S(1)} copy-done((bf16[128,2048]{1,0:T(8,128)(2,1)S(1)}, bf16[128,2048]{1,0:T(8,128)(2,1)}, u32[]{:S(2)}) %copy-start.2) | copy-done | bytes 524312
  3.1 0.0 copy-start.3
  3.1 0.9 %copy-done.3 = bf16[64,2048]{1,0:T(8,128)(2,1)S(1)} copy-done((bf16[64,2048]{1,0:T(8,128)(2,1)S(1)}, bf16[64,2048]{1,0:T(8,128)(2,1)}, u32[]{:S(2)}) %copy-start.3) | copy-done | bytes 262168
  4.1 0.0 copy-start.4
  4.1 0.7 %copy-done.4 = bf16[128,16]{0,1:T(8,128)(2,1)S(1)} copy-done((bf16[128,16]{0,1:T(8,128)(2,1)S(1)}, bf16[128,16]{0,1:T(8,128)(2,1)}, u32[]{:S(2)}) %copy-start.4) | copy-done | bytes 4120
  4.8 54.1 %shard_map.55 = bf16[128,2048]{1,0:T(8,128)(2,1)S(1)} custom-call(bf16[128,2048]{1,0:T(8,128)(2,1)S(1)} %copy-done, bf16[128,2048]{1,0:T(8,128)(2,1)S(1)} %copy-done.1, bf16[128,2048]{1,0:T(8,128)(2,1)S(1)} %copy-done.2, bf16[16,128]{1,0:T(8,128)(2,1)S(1)} %bitcast.1, bf16[64,2048]{1,0:T(8,128)(2,1)S(1)} %copy-done.3), custom_call_target="tpu_custom_call" | custom-call | tf_op jit(solution)/shard_map/pallas_call | solution.py:367
  58.9 0.8 %copy.7 = bf16[128,2048]{1,0:T(8,128)(2,1)} copy(bf16[128,2048]{1,0:T(8,128)(2,1)S(1)} %shard_map.55) | data formatting | bytes 1048576
Async XLA Ops:
  0.0 1.0 %copy-start = (bf16[128,2048]{1,0:T(8,128)(2,1)S(1)}, bf16[128,2048]{1,0:T(8,128)(2,1)}, u32[]{:S(2)}) copy-start(bf16[128,2048]{1,0:T(8,128)(2,1)} %refs_0_.1) | copy-start | bytes 1572868
  1.0 1.0 %copy-start.1 = (bf16[128,2048]{1,0:T(8,128)(2,1)S(1)}, bf16[128,2048]{1,0:T(8,128)(2,1)}, u32[]{:S(2)}) copy-start(bf16[128,2048]{1,0:T(8,128)(2,1)} %refs_1_.1) | copy-start | bytes 1572868
  2.1 1.0 %copy-start.2 = (bf16[128,2048]{1,0:T(8,128)(2,1)S(1)}, bf16[128,2048]{1,0:T(8,128)(2,1)}, u32[]{:S(2)}) copy-start(bf16[128,2048]{1,0:T(8,128)(2,1)} %refs_2_.1) | copy-start | bytes 1572868
  3.1 0.9 %copy-start.3 = (bf16[64,2048]{1,0:T(8,128)(2,1)S(1)}, bf16[64,2048]{1,0:T(8,128)(2,1)}, u32[]{:S(2)}) copy-start(bf16[64,2048]{1,0:T(8,128)(2,1)} %refs_4_.1) | copy-start | bytes 786436
  4.1 0.7 %copy-start.4 = (bf16[128,16]{0,1:T(8,128)(2,1)S(1)}, bf16[128,16]{0,1:T(8,128)(2,1)}, u32[]{:S(2)}) copy-start(bf16[128,16]{0,1:T(8,128)(2,1)} %param.8) | copy-start | bytes 12292
